TPU v7x, 1024 devices: a whole 4x4x32 slice. The times are simulated.
1024 devices in a mesh: hst: 64 (over z, core), dev: 16 (over x, y).
Axes of the slice: x: 4, y: 4, z: 32, core: 2. Of those that a mesh axis runs over, the one named last changes fastest.
Arguments:
- cache_table: bfloat16 [1024, 512], P('dev'), may hold values from -6 to 6
- cold_table: bfloat16 [262144, 512], P(('hst', 'dev')), may hold values from -6 to 6
- hit_ids: int32 [16384, 32], P(('hst', 'dev')), may hold values from 0 to 63
- miss_owner: int32 [262144, 1], P(('hst', 'dev')), may hold values from 0 to 63; in each aligned block of 256 rows (0 to 255, 256 to 511, ...) at most 8 rows name the same one
- miss_row: int32 [262144], P(('hst', 'dev')), may hold values from 0 to 255
- history_ids: int32 [2048, 512], P(('hst', 'dev')), may hold values from 0 to 767
- candidate_ids: int32 [2048, 128], P(('hst', 'dev')), may hold values from 0 to 767
- history_len: int32 [2048], P(('hst', 'dev')), may hold values from 64 to 512
- w_kv: bfloat16 [512, 1024], replicated, may hold values from -0.25 to 0.25
- w_cand: bfloat16 [512, 2048], replicated, may hold values from -0.25 to 0.25
- w_out: bfloat16 [512, 512], replicated, may hold values from -0.25 to 0.25
- w_score: float32 [512], replicated, may hold values from -0.25 to 0.25
Outputs:
- scores: float32 [2048, 128], P(('hst', 'dev'))
Inputs may be any that keep to these rules, and one draw needn't show every extreme that they name: `hit_ids`: each id names a row of the cache shard held by the device of the asker's host group whose index along dev is the id's row number modulo the size of dev. `miss_owner`: a missed row lies in the cold shard of the owner group's device that has the asker's index along dev; each device names one group at most 8 times.
All inputs are finite; a program needn't handle non-finite values.
Results may differ from a plain program's by a relative error of at most 0.0039.
Values may be sent and summed in bfloat16 or wider, within the bound.
A program may use at most 32 MiB of HBM per device.

v0:
```python
import math

import jax
import jax.numpy as jnp
from jax import lax
from jax.sharding import PartitionSpec as P

D = 512
HEADS = 4
DH = 128
MISS_CAP = 8


def normalize(values):
    mean = jnp.mean(values, axis=-1, keepdims=True)
    centered = values - mean
    var = jnp.mean(centered * centered, axis=-1, keepdims=True)
    return centered / jnp.sqrt(var + 1e-05)


def project_keys(rows_x, w_kv):
    normed = normalize(rows_x.astype(jnp.float32)).astype(jnp.bfloat16)
    return jax.nn.silu(
        jnp.einsum("uld,de->ule", normed, w_kv, preferred_element_type=jnp.float32)
    ).astype(jnp.bfloat16)


def block_terms(query, kv, live):
    users, span = (kv.shape[0], kv.shape[1])
    keys = kv[..., :D].reshape(users, span, HEADS, DH)
    values = kv[..., D:].reshape(users, span, HEADS, DH)
    raw = jnp.einsum("uchd,ulhd->uhcl", query, keys, preferred_element_type=jnp.float32) * (
        1.0 / math.sqrt(DH)
    )
    weight = (jax.nn.silu(raw) * live[:, None, None, :]).astype(jnp.bfloat16)
    return jnp.einsum("uhcl,ulhd->uchd", weight, values, preferred_element_type=jnp.float32)


def per_device(
    cache_table,
    cold_table,
    hit_ids,
    miss_owner,
    miss_row,
    history_ids,
    candidate_ids,
    history_len,
    w_kv,
    w_cand,
    w_out,
    w_score,
):
    width = cache_table.shape[1]
    n_hst = lax.axis_size("hst")
    arrived_hits = lax.all_to_all(
        jnp.take(
            cache_table,
            lax.all_to_all(hit_ids, "dev", split_axis=0, concat_axis=0, tiled=True),
            axis=0,
        ),
        "dev",
        split_axis=0,
        concat_axis=0,
        tiled=True,
    )
    hit_rows = arrived_hits.reshape(-1, width)
    owners = miss_owner[:, 0]
    onehot = (owners[:, None] == jnp.arange(n_hst, dtype=jnp.int32)[None, :]).astype(jnp.int32)
    before = jnp.cumsum(onehot, axis=0) - onehot
    slot = jnp.sum(before * onehot, axis=1)
    request = jnp.zeros((n_hst, MISS_CAP), jnp.int32).at[owners, slot].set(miss_row)
    arrived_misses = lax.all_to_all(
        jnp.take(
            cold_table,
            lax.all_to_all(request, "hst", split_axis=0, concat_axis=0, tiled=True),
            axis=0,
        ),
        "hst",
        split_axis=0,
        concat_axis=0,
        tiled=True,
    )
    miss_rows = arrived_misses[owners, slot]
    collected = jnp.concatenate([hit_rows, miss_rows], axis=0)
    users, hist = history_ids.shape
    cands = candidate_ids.shape[1]
    history_x = jnp.take(collected, history_ids, axis=0)
    cand_x = jnp.take(collected, candidate_ids, axis=0)
    cand_n = normalize(cand_x.astype(jnp.float32)).astype(jnp.bfloat16)
    proj = jax.nn.silu(
        jnp.einsum("ucd,de->uce", cand_n, w_cand, preferred_element_type=jnp.float32)
    ).astype(jnp.bfloat16)
    gate = proj[..., :D]
    cand_value = proj[..., D : 2 * D].reshape(users, cands, HEADS, DH)
    query = proj[..., 2 * D : 3 * D].reshape(users, cands, HEADS, DH)
    cand_key = proj[..., 3 * D :].reshape(users, cands, HEADS, DH)
    live = (jnp.arange(hist, dtype=jnp.int32)[None, :] < history_len[:, None]).astype(jnp.float32)
    summed = block_terms(query, project_keys(history_x, w_kv), live)
    own = jnp.einsum("uchd,uchd->uch", query, cand_key, preferred_element_type=jnp.float32) * (
        1.0 / math.sqrt(DH)
    )
    attended = summed / history_len.astype(jnp.float32)[:, None, None, None] + jax.nn.silu(own)[
        ..., None
    ] * cand_value.astype(jnp.float32)
    attended = attended.reshape(users, cands, D)
    mixed = (normalize(attended) * gate.astype(jnp.float32)).astype(jnp.bfloat16)
    branch = jnp.dot(
        mixed.reshape(users * cands, D), w_out, preferred_element_type=jnp.float32
    ).reshape(users, cands, D)
    output = cand_x.astype(jnp.float32) + branch
    return jnp.sum(output * w_score, axis=-1)


def solution(mesh):
    placed = (
        P("dev", None),
        P(("hst", "dev"), None),
        P(("hst", "dev"), None),
        P(("hst", "dev"), None),
        P(("hst", "dev")),
        P(("hst", "dev"), None),
        P(("hst", "dev"), None),
        P(("hst", "dev")),
        P(),
        P(),
        P(),
        P(),
    )
    return jax.shard_map(
        per_device, mesh=mesh, in_specs=placed, out_specs=P(("hst", "dev"), None), check_vma=False
    )
```

profile of v0, /device:TPU:1, one launch (start us, length us, event | category | flops | bytes accessed | tf_op | source)
XLA Modules:
  0.0 201.1 jit_solution(1186024154694509904)
XLA Ops:
  0.0 0.8 fusion.41
  0.8 0.6 reduce-window.6
  1.7 0.8 fusion.40
  2.5 0.7 or_select_fusion
  3.2 21.2 %scatter_fusion = s32[64,8]{0,1:T(8,128)S(1)} fusion(s32[64,8]{0,1:T(8,128)S(1)} %broadcast_in_dim.69, s32[256]{0:T(256)S(1)} %bitcast.87, s32[256]{0:T(256)} %param.16), kind=kCustom, calls=%fused_computation.5 | custom fusion | bytes 5120 | tf_op jit(solution)/shard_map/scatter | solution.py:71
  24.5 52.6 %all_to_all.40 = s32[64,1,8]{2,1,0:T(1,128)S(1)} all-to-all(s32[64,1,8]{2,1,0:T(1,128)S(1)} %copy.28), channel_id=1, replica_groups=mesh['hst'=64,'dev'=16] {'hst'}, dimensions={0} | all-to-all | bytes 4096 | tf_op jit(solution)/shard_map/all_to_all | solution.py:75
  77.1 6.8 %all-to-all-start = ((s32[16,1,32]{2,1,0:T(1,128)}), s32[16,1,32]{2,1,0:T(1,128)S(1)}, u32[]{:S(2)}, u32[]{:S(2)}) async-start(s32[16,1,32]{2,1,0:T(1,128)} %bitcast), calls=%async_computation | async-start | bytes 16384 | tf_op jit(solution)/shard_map/all_to_all | solution.py:58
  84.2 2.0 gather_fusion.1
  86.2 0.9 bitcast_select_fusion
  87.2 3.0 %all-to-all-done = s32[16,1,32]{2,1,0:T(1,128)S(1)} async-done(((s32[16,1,32]{2,1,0:T(1,128)}), s32[16,1,32]{2,1,0:T(1,128)S(1)}, u32[]{:S(2)}, u32[]{:S(2)}) %all-to-all-start) | async-done | bytes 2080 | tf_op jit(solution)/shard_map/all_to_all | solution.py:58
  90.2 7.1 %all-to-all-start.3 = ((bf16[64,8,512]{2,1,0:T(8,128)(2,1)}), bf16[64,8,512]{2,1,0:T(8,128)(2,1)S(1)}, u32[]{:S(2)}, u32[]{:S(2)}) async-start(bf16[64,8,512]{2,1,0:T(8,128)(2,1)} %bitcast_select_fusion), calls=%async_computation.3 | async-start | bytes 1048576 | tf_op jit(solution)/shard_map/all_to_all | solution.py:72
  97.5 2.0 gather_fusion
  99.5 0.9 broadcast_select_fusion.2
  100.5 61.2 %all-to-all-done.3 = bf16[64,8,512]{2,1,0:T(8,128)(2,1)S(1)} async-done(((bf16[64,8,512]{2,1,0:T(8,128)(2,1)}), bf16[64,8,512]{2,1,0:T(8,128)(2,1)S(1)}, u32[]{:S(2)}, u32[]{:S(2)}) %all-to-all-start.3) | async-done | bytes 524320 | tf_op jit(solution)/shard_map/all_to_all | solution.py:72
  161.7 3.8 %all-to-all-start.1 = ((bf16[16,32,512]{2,1,0:T(8,128)(2,1)}), bf16[16,32,512]{2,1,0:T(8,128)(2,1)S(1)}, u32[]{:S(2)}, u32[]{:S(2)}) async-start(bf16[16,32,512]{2,1,0:T(8,128)(2,1)} %broadcast_select_fusion.2), calls=%async_computation.1 | async-start | bytes 1048576 | tf_op jit(solution)/shard_map/all_to_all | solution.py:55
  165.5 2.7 %gather_fusion.2 = bf16[256,512]{1,0:T(8,128)(2,1)} fusion(bf16[64,8,512]{2,1,0:T(8,128)(2,1)S(1)} %all-to-all-done.3, s32[256]{0:T(256)S(1)} %bitcast.86), kind=kCustom, calls=%fused_computation.2 | custom fusion | bytes 526336 | tf_op jit(solution)/shard_map/gather | solution.py:83
  168.3 7.3 %all-to-all-done.1 = bf16[16,32,512]{2,1,0:T(8,128)(2,1)S(1)} async-done(((bf16[16,32,512]{2,1,0:T(8,128)(2,1)}), bf16[16,32,512]{2,1,0:T(8,128)(2,1)S(1)}, u32[]{:S(2)}, u32[]{:S(2)}) %all-to-all-start.1) | async-done | bytes 524320 | tf_op jit(solution)/shard_map/all_to_all | solution.py:55
  175.6 1.0 pad_maximum_fusion
  176.6 1.2 gather_fusion.3
  178.0 0.2 fusion.22
  178.2 5.1 %gather_fusion.4 = bf16[1024,512]{1,0:T(8,128)(2,1)} fusion(bf16[768,512]{1,0:T(8,128)(2,1)S(1)} %pad_maximum_fusion, s32[1024]{0:T(1024)S(1)} %broadcast_clamp_fusion), kind=kCustom, calls=%fused_computation.4 | custom fusion | bytes 2101248 | tf_op jit(solution)/shard_map/jit(_take)/gather | solution.py:87
  183.3 1.8 convert_reduce_fusion
  185.1 1.9 fusion.2
  187.1 2.2 %multiply_convert_fusion = bf16[2,512,1024]{2,1,0:T(8,128)(2,1)S(1)} fusion(bf16[512,1024]{1,0:T(8,128)(2,1)S(1)} %copy-done.8, f32[2,512]{1,0:T(2,128)S(1)} %add_sqrt_fusion, f32[2,512]{1,0:T(2,128)S(1)} %broadcast_multiply_fusion, bf16[2,512,512]{2,1,0:T(8,128)(2,1)S(1)} %bitcast.90, pred[2,512]{1,0:T(4,128)(4,1)S(1)} %compare_and_fusion), kind=kOutput, calls=%fused_computation.6 | convolution fusion | flops 1081606144 | bytes 4203520 | tf_op jit(solution)/shard_map/uld,de->ule/dot_general | solution.py:24
  189.2 1.3 slice_bitcast_fusion
  190.6 1.3 copy.41
  191.9 0.9 multiply_convert_fusion.2
  192.8 1.0 fusion.50
  194.0 1.0 reshape.196
  195.0 0.4 fusion.25
  195.7 2.9 %fusion.51 = (f32[2,128]{1,0:T(2,128)S(1)}, f32[2,128,4,128]{1,3,2,0:T(8,128)S(1)}) fusion(f32[2,128,4,128]{1,3,2,0:T(8,128)S(1)} %bitcast.99, f32[2,128,4]{1,2,0:T(4,128)S(1)} %divide_multiply_fusion, f32[2]{0:T(128)S(1)} %convert_element_type.61, bf16[2,512,4,128]{1,3,2,0:T(8,128)(2,1)} %bitcast.98, bf16[2,64,4,8,128]{4,3,2,1,0:T(8,128)(2,1)} %get-tuple-element.7, ...), kind=kOutput, calls=%fused_computation.100 | convolution fusion | flops 272629504 | bytes 3417096 | tf_op jit(solution)/shard_map/uhcl,ulhd->uchd/dot_general | solution.py:36
  198.9 2.1 %fusion.11 = f32[2,128]{1,0:T(2,128)} fusion(bf16[512,512]{1,0:T(8,128)(2,1)} %param.22, f32[2,128,512]{2,1,0:T(8,128)S(1)} %copy.44, bf16[2,128,2048]{2,1,0:T(8,128)(2,1)} %copy-done.4, f32[512]{0:T(512)S(1)} %copy-done.9, f32[2,128]{1,0:T(2,128)S(1)} %add_sqrt_fusion.1, f32[2,128]{1,0:T(2,128)S(1)} %broadcast_multiply_fusion.1, ...), kind=kOutput, calls=%fused_computation.22 | convolution fusion | flops 135528192 | bytes 1578240 | tf_op jit(solution)/shard_map/dot_general | solution.py:107
  (57 shorter events, 1.8 us)
Async XLA Ops:
  0.0 191.9 %copy-start = (bf16[512,2048]{1,0:T(8,128)(2,1)S(1)}, bf16[512,2048]{1,0:T(8,128)(2,1)}, u32[]{:S(2)}) copy-start(bf16[512,2048]{1,0:T(8,128)(2,1)} %param.21) | copy-start | bytes 6291460
  0.0 84.2 %copy-start.2 = (bf16[256,512]{1,0:T(8,128)(2,1)S(1)}, bf16[256,512]{1,0:T(8,128)(2,1)}, u32[]{:S(2)}) copy-start(bf16[256,512]{1,0:T(8,128)(2,1)} %param.13) | copy-start | bytes 786436
  77.1 13.1 %all-to-all-start = ((s32[16,1,32]{2,1,0:T(1,128)}), s32[16,1,32]{2,1,0:T(1,128)S(1)}, u32[]{:S(2)}, u32[]{:S(2)}) async-start(s32[16,1,32]{2,1,0:T(1,128)} %bitcast), calls=%async_computation | async-start | bytes 16384 | tf_op jit(solution)/shard_map/all_to_all | solution.py:58
  86.2 11.2 %copy-start.6 = (s32[2,128]{1,0:T(2,128)S(1)}, s32[2,128]{1,0:T(2,128)}, u32[]{:S(2)}) copy-start(s32[2,128]{1,0:T(2,128)} %param.18) | copy-start | bytes 3076
  86.2 11.2 %copy-start.7 = (s32[2]{0:T(128)S(1)}, s32[2]{0:T(128)}, u32[]{:S(2)}) copy-start(s32[2]{0:T(128)} %param.19) | copy-start | bytes 28
  86.2 11.2 %copy-start.5 = (s32[2,512]{1,0:T(2,128)S(1)}, s32[2,512]{1,0:T(2,128)}, u32[]{:S(2)}) copy-start(s32[2,512]{1,0:T(2,128)} %param.17) | copy-start | bytes 12292
  86.2 11.3 %copy-start.1 = (bf16[64,512]{1,0:T(8,128)(2,1)S(1)}, bf16[64,512]{1,0:T(8,128)(2,1)}, u32[]{:S(2)}) copy-start(bf16[64,512]{1,0:T(8,128)(2,1)} %param.12) | copy-start | bytes 196612
  90.2 71.5 %all-to-all-start.3 = ((bf16[64,8,512]{2,1,0:T(8,128)(2,1)}), bf16[64,8,512]{2,1,0:T(8,128)(2,1)S(1)}, u32[]{:S(2)}, u32[]{:S(2)}) async-start(bf16[64,8,512]{2,1,0:T(8,128)(2,1)} %bitcast_select_fusion), calls=%async_computation.3 | async-start | bytes 1048576 | tf_op jit(solution)/shard_map/all_to_all | solution.py:72
  161.7 13.9 %all-to-all-start.1 = ((bf16[16,32,512]{2,1,0:T(8,128)(2,1)}), bf16[16,32,512]{2,1,0:T(8,128)(2,1)S(1)}, u32[]{:S(2)}, u32[]{:S(2)}) async-start(bf16[16,32,512]{2,1,0:T(8,128)(2,1)} %broadcast_select_fusion.2), calls=%async_computation.1 | async-start | bytes 1048576 | tf_op jit(solution)/shard_map/all_to_all | solution.py:55
  183.3 3.7 %copy-start.3 = (bf16[1024,512]{1,0:T(8,128)(2,1)S(1)}, bf16[1024,512]{1,0:T(8,128)(2,1)}, u32[]{:S(2)}) copy-start(bf16[1024,512]{1,0:T(8,128)(2,1)} %gather_fusion.4) | copy-start | bytes 3145732
  183.3 3.7 %copy-start.8 = (bf16[512,1024]{1,0:T(8,128)(2,1)S(1)}, bf16[512,1024]{1,0:T(8,128)(2,1)}, u32[]{:S(2)}) copy-start(bf16[512,1024]{1,0:T(8,128)(2,1)} %param.20) | copy-start | bytes 3145732
  192.8 1.1 copy-start.4
  195.7 3.2 %copy-start.9 = (f32[512]{0:T(512)S(1)}, f32[512]{0:T(512)}, u32[]{:S(2)}) copy-start(f32[512]{0:T(512)} %param.23) | copy-start | bytes 6148
where the time goes:
time: 202 us; the launch traced here: 201 us
  waiting for transfers between devices  71.6 us (35%)
  blocking collectives  52.6 us (26%)
  local copies, waits for them, and re-layouts  39.1 us (19%)
  starting transfers between devices  17.6 us (9%)
  other arithmetic  11.7 us (6%)
  matrix products  8.07 us (4%)
    all_to_all x1, waiting for transfers between devices, per_device(): lax.all_to_all(jnp.take(cold_table, lax.all_to_all(request, 'hst', split_...  61.2 us
    all_to_all x1, blocking collectives, per_device(): lax.all_to_all(request, 'hst', split_axis=0, concat_axis=0, tiled=True)  52.6 us
    scatter x1, local copies, waits for them, and re-layouts, per_device(): jnp.zeros((n_hst, MISS_CAP), jnp.int32).at[owners, slot].set(miss_row)  21.2 us
    all_to_all x1, waiting for transfers between devices, per_device(): lax.all_to_all(jnp.take(cache_table, lax.all_to_all(hit_ids, 'dev', split...  7.34 us
    all_to_all x1, starting transfers between devices, per_device(): lax.all_to_all(jnp.take(cold_table, lax.all_to_all(request, 'hst', split_...  7.09 us
    all_to_all x1, starting transfers between devices, per_device(): lax.all_to_all(hit_ids, 'dev', split_axis=0, concat_axis=0, tiled=True)  6.76 us
    gather x1, local copies, waits for them, and re-layouts, per_device(): history_x = jnp.take(collected, history_ids, axis=0)  5.07 us
  transfers between devices with their start and end apart: 3, of which 3 were waited for; matrix products, arithmetic and copies ran while one was open for 4% of the time, Pallas kernels for 0%

commit v1 on v0

v1 whole, which is shorter than its diff:
```python
import functools
import math

import jax
import jax.numpy as jnp
from jax import lax
from jax.experimental import pallas as pl
from jax.experimental.pallas import tpu as pltpu
from jax.sharding import PartitionSpec as P

F32 = jnp.float32
BF16 = jnp.bfloat16
HEADS = 4
DH = 128
CAP = 8
EPS = 1e-05


def iota(shape, dim):
    return lax.broadcasted_iota(jnp.int32, shape, dim)


def normalize(x):
    centered = x - jnp.mean(x, axis=-1, keepdims=True)
    var = jnp.mean(centered * centered, axis=-1, keepdims=True)
    return centered * lax.rsqrt(var + EPS)


def silu_of_double(y):
    return y + y * jnp.tanh(y)


def dot(a, b):
    return jnp.dot(a, b, preferred_element_type=F32)


def dot_nt(a, b):
    return lax.dot_general(a, b, (((1,), (1,)), ((), ())), preferred_element_type=F32)


def columns(rows):
    r, n = rows.shape
    eye = iota((n, n), 0) == iota((n, n), 1)
    spread = jnp.where(eye[None], jnp.broadcast_to(rows[:, None, :], (r, n, n)), 0.0)
    return jnp.sum(spread, axis=-1, keepdims=True).reshape(r * n, 1)


def onehot(column, width):
    lanes = iota((column.shape[0], width), 1).astype(F32)
    return jnp.where(column == lanes, 1.0, 0.0).astype(BF16)


def kernel(
    n_hst,
    n_dev,
    cache,
    cold,
    hit_ids,
    owner,
    miss_row,
    history_ids,
    candidate_ids,
    history_len,
    w_kv_hbm,
    w_cand_hbm,
    w_out_hbm,
    w_score,
    out,
    w_kv,
    w_cand,
    w_out,
    asked,
    request,
    reply,
    arrived,
    cached,
    kv,
    w_sem,
    ask_send,
    ask_recv,
    row_send,
    row_recv,
    ag_send,
    ag_recv,
    swap_send,
    swap_recv,
):
    me = lax.axis_index("hst")
    dev = lax.axis_index("dev")
    z, core = me // 2, lax.rem(me, 2)
    nz = n_hst // 2
    far = nz // 2
    hits = hit_ids.shape[0] * hit_ids.shape[1]
    misses = owner.shape[0] * owner.shape[1]
    width = cache.shape[1]
    half_w = width // 2
    half = cache.shape[0] // 2
    chunk = n_hst // row_recv.shape[0]
    chunks = n_hst // chunk

    def group_at(k, sign):
        pair = k // 2
        step = (far - (pair + 1) // 2) * (2 * lax.rem(pair, 2) - 1)
        chip = lax.rem(z + sign * step + nz, nz)
        return chip * 2 + lax.rem(core + 1 - lax.rem(k, 2), 2)

    weights = [
        pltpu.make_async_copy(w_kv_hbm, w_kv, w_sem.at[0]),
        pltpu.make_async_copy(w_cand_hbm, w_cand, w_sem.at[1]),
        pltpu.make_async_copy(w_out_hbm, w_out, w_sem.at[2]),
    ]

    barrier = pltpu.get_barrier_semaphore()

    def greet_group(k, carry):
        pl.semaphore_signal(barrier, inc=1, device_id={"hst": group_at(k, 1), "dev": dev})
        return carry

    def greet_dev(k, carry):
        pl.semaphore_signal(barrier, inc=1, device_id={"hst": me, "dev": lax.rem(dev + k, n_dev)})
        return carry

    lax.fori_loop(0, n_hst - 1, greet_group, 0)
    lax.fori_loop(1, n_dev, greet_dev, 0)
    for w in weights:
        w.start()

    owners = owner[...].astype(F32)
    owner_col = columns(owners)
    row_col = columns(miss_row[...].astype(F32))
    by_miss = onehot(owner_col, 128)
    earlier = jnp.where(iota((misses, misses), 1) < iota((misses, misses), 0), 1.0, 0.0).astype(BF16)
    before = dot(earlier, by_miss)
    slot_col = jnp.sum(before * by_miss.astype(F32), axis=-1, keepdims=True)
    lanes = iota((misses, 128), 1).astype(F32)
    rows_at_slot = jnp.where(slot_col == lanes, row_col, 0.0).astype(BF16)
    wanted = jnp.zeros((n_hst, 128), F32)
    groups = iota((n_hst, 128), 0).astype(F32)
    for i in range(misses // 128):
        by_group = jnp.where(owners[i : i + 1] == groups, 1.0, 0.0).astype(BF16)
        wanted = wanted + dot(by_group, rows_at_slot[i * 128 : (i + 1) * 128])
    asked[...] = wanted.reshape(n_hst, 1, 128)
    request[n_hst - 1] = asked[me]

    pl.semaphore_wait(barrier, n_hst - 1 + n_dev - 1)

    def ask(k, carry):
        to = group_at(k, 1)
        pltpu.make_async_remote_copy(
            src_ref=asked.at[to],
            dst_ref=request.at[k],
            send_sem=ask_send,
            recv_sem=ask_recv,
            device_id={"hst": to, "dev": dev},
        ).start()
        return carry

    lax.fori_loop(0, n_hst - 1, ask, 0)

    def share(k, carry):
        pltpu.make_async_remote_copy(
            src_ref=cache.at[pl.ds(pl.multiple_of(core * half, half), half)],
            dst_ref=cached.at[core, k],
            send_sem=ag_send,
            recv_sem=ag_recv,
            device_id={"hst": me, "dev": lax.rem(dev + k, n_dev)},
        ).start()
        return carry

    lax.fori_loop(1, n_dev, share, 0)

    collected = hits + misses
    users = history_len.shape[0]
    hist = history_ids.shape[1]
    counts = []
    for u in range(users):
        ids = history_ids[u : u + 1, :].astype(F32)
        ids = jnp.where(iota((1, hist), 1) < history_len[u], ids, -1.0)
        col = jnp.concatenate([columns(ids[:, i * 128 : (i + 1) * 128]) for i in range(hist // 128)], axis=0)
        same = col == iota((hist, collected), 1).astype(F32)
        counts.append(jnp.sum(jnp.where(same, 1.0, 0.0), axis=0, keepdims=True))
    cand_col = columns(candidate_ids[...].astype(F32))
    of_hits = onehot(cand_col, hits)
    of_misses = onehot(cand_col - float(hits), misses)

    all_but_self = pl.ds(0, n_hst - 1)
    own_group = {"hst": me, "dev": dev}

    def whole(ref, sem_send, sem_recv):
        return pltpu.make_async_remote_copy(
            src_ref=ref, dst_ref=ref, send_sem=sem_send, recv_sem=sem_recv, device_id=own_group
        )

    whole(request.at[all_but_self], ask_send, ask_recv).wait_recv()

    def answer(i, carry):
        ids = request[pl.ds(i * chunk, chunk)]
        pick = iota((chunk, CAP, 128), 1) == iota((chunk, CAP, 128), 2)
        spread = jnp.where(pick, jnp.broadcast_to(ids, (chunk, CAP, 128)), 0.0)
        col = jnp.sum(spread, axis=-1, keepdims=True).reshape(chunk * CAP, 1)
        rows = dot(onehot(col, cold.shape[0]), cold[...]).astype(BF16)
        rows = rows.reshape(chunk, CAP, width)
        reply[pl.ds(i * chunk, chunk), 0:CAP, :] = rows[:, :, :half_w]
        reply[pl.ds(i * chunk, chunk), CAP:, :] = rows[:, :, half_w:]

        def send(k, inner):
            pltpu.make_async_remote_copy(
                src_ref=reply.at[k],
                dst_ref=arrived.at[k],
                send_sem=row_send,
                recv_sem=row_recv.at[i],
                device_id={"hst": group_at(k, -1), "dev": dev},
            ).start()
            return inner

        return lax.fori_loop(i * chunk, jnp.minimum((i + 1) * chunk, n_hst - 1), send, carry)

    lax.fori_loop(0, chunks, answer, 0)
    arrived[n_hst - 1] = reply[n_hst - 1]

    others = pl.ds(1, n_dev - 1)
    whole(cached.at[core, others], ag_send, ag_recv).wait_recv()
    swap = pltpu.make_async_remote_copy(
        src_ref=cached.at[core, others],
        dst_ref=cached.at[core, others],
        send_sem=swap_send,
        recv_sem=swap_recv,
        device_id={"hst": z * 2 + 1 - core, "dev": dev},
    )
    swap.start()
    cached[0, 0] = cache[0:half]
    cached[1, 0] = cache[half:]
    for w in weights:
        w.wait()
    heads_col = jnp.sum(w_out[...].astype(F32) * w_score[...], axis=-1, keepdims=True)
    eye = iota((128, 128), 0) == iota((128, 128), 1)
    head_row = jnp.concatenate(
        [
            jnp.sum(jnp.where(eye, heads_col[i * 128 : (i + 1) * 128], 0.0), axis=0, keepdims=True)
            for i in range(width // 128)
        ],
        axis=1,
    )
    peers, slots = hit_ids.shape
    ids = hit_ids[...]
    peer = iota((peers, slots), 0)
    place = (ids // half) * (peers * half) + lax.rem(dev - peer + peers, peers) * half + lax.rem(ids, half)
    spread = jnp.where(
        (iota((slots, slots), 0) == iota((slots, slots), 1))[None],
        jnp.broadcast_to(place.astype(F32)[:, None, :], (peers, slots, slots)),
        0.0,
    )
    place_col = jnp.sum(spread, axis=-1, keepdims=True).reshape(hits, 1)
    whole(cached.at[1 - core, others], swap_send, swap_recv).wait_recv()
    x_hit = dot(onehot(place_col, 2 * peers * half), cached[...].reshape(2 * peers * half, width)).astype(BF16)
    normed = normalize(x_hit.astype(F32)).astype(BF16)
    kv[0:hits] = silu_of_double(0.5 * dot(normed, w_kv[...])).astype(BF16)
    cand_x = dot(of_hits, x_hit)

    o = owner_col.astype(jnp.int32)
    chip = lax.rem(o // 2 - z + nz, nz)
    pair = jnp.where(chip >= far, 2 * (chip - far), 2 * (far - chip) - 1)
    order = 2 * pair + 1 - lax.rem(o + core, 2)
    seat_col = (order * CAP).astype(F32) + slot_col
    left = jnp.zeros((misses, half_w), F32)
    right = jnp.zeros((misses, half_w), F32)
    for i in range(chunks):
        n = chunk - (i == chunks - 1)
        whole(arrived.at[pl.ds(i * chunk, n)], row_send, row_recv.at[i]).wait_recv()
        pick = onehot(seat_col - float(i * chunk * CAP), chunk * CAP)
        part = arrived[pl.ds(i * chunk, chunk)]
        left = left + dot(pick, part[:, 0:CAP, :].reshape(chunk * CAP, half_w))
        right = right + dot(pick, part[:, CAP:, :].reshape(chunk * CAP, half_w))
    x_miss32 = jnp.concatenate([left, right], axis=1)
    x_miss = x_miss32.astype(BF16)
    cand_x = cand_x + dot(of_misses, x_miss)
    normed = normalize(x_miss32).astype(BF16)
    kv[hits:] = silu_of_double(0.5 * dot(normed, w_kv[...])).astype(BF16)

    cand_n = normalize(cand_x).astype(BF16)
    proj = silu_of_double(0.5 * dot(cand_n, w_cand[...])).astype(BF16)
    cands = candidate_ids.shape[1]
    scale = 1.0 / math.sqrt(DH)
    attended = []
    for h in range(HEADS):
        cols = slice(h * DH, (h + 1) * DH)
        at = lambda b: proj[:, b * width + h * DH : b * width + (h + 1) * DH]
        query = at(2)
        half_raw = dot_nt(query, kv[:, cols]) * (0.5 * scale)
        act = silu_of_double(half_raw)
        weight = jnp.concatenate(
            [(act[u * cands : (u + 1) * cands] * counts[u]).astype(BF16) for u in range(users)], axis=0
        )
        summed = dot(weight, kv[:, width + h * DH : width + (h + 1) * DH])
        own = jnp.sum(query.astype(F32) * at(3).astype(F32), axis=-1, keepdims=True) * (0.5 * scale)
        mine = silu_of_double(own) * at(1).astype(F32)
        shares = [
            summed[u * cands : (u + 1) * cands] / history_len[u].astype(F32) for u in range(users)
        ]
        attended.append(jnp.concatenate(shares, axis=0) + mine)
    mixed = normalize(jnp.concatenate(attended, axis=1)) * proj[:, :width].astype(F32)
    score = jnp.sum(cand_x * w_score[...] + mixed * head_row, axis=-1, keepdims=True)
    eye = iota((cands, cands), 0) == iota((cands, cands), 1)
    for u in range(users):
        out[u : u + 1, :] = jnp.sum(
            jnp.where(eye, score[u * cands : (u + 1) * cands], 0.0), axis=0, keepdims=True
        )

    whole(asked.at[all_but_self], ask_send, ask_recv).wait_send()
    whole(reply.at[all_but_self], row_send, row_recv.at[0]).wait_send()
    whole(cached.at[core, others], ag_send, ag_recv).wait_send()
    swap.wait_send()


def per_device(
    n_hst,
    n_dev,
    cache_table,
    cold_table,
    hit_ids,
    miss_owner,
    miss_row,
    history_ids,
    candidate_ids,
    history_len,
    w_kv,
    w_cand,
    w_out,
    w_score,
):
    width = cache_table.shape[1]
    misses = miss_row.shape[0]
    collected = hit_ids.size + misses
    half = cache_table.shape[0] // 2
    chunks = 4
    vmem = pl.BlockSpec(memory_space=pltpu.VMEM)
    smem = pl.BlockSpec(memory_space=pltpu.SMEM)
    hbm = pl.BlockSpec(memory_space=pl.ANY)
    dma = pltpu.SemaphoreType.DMA
    return pl.pallas_call(
        functools.partial(kernel, n_hst, n_dev),
        out_shape=jax.ShapeDtypeStruct(candidate_ids.shape, F32),
        in_specs=[vmem] * 7 + [smem] + [hbm] * 3 + [vmem],
        out_specs=vmem,
        scratch_shapes=[
            pltpu.VMEM(w_kv.shape, BF16),
            pltpu.VMEM(w_cand.shape, BF16),
            pltpu.VMEM(w_out.shape, BF16),
            pltpu.VMEM((n_hst, 1, 128), F32),
            pltpu.VMEM((n_hst, 1, 128), F32),
            pltpu.VMEM((n_hst, 2 * CAP, width // 2), BF16),
            pltpu.VMEM((n_hst, 2 * CAP, width // 2), BF16),
            pltpu.VMEM((2, n_dev, half, width), BF16),
            pltpu.VMEM((collected, 2 * width), BF16),
            dma((3,)),
            dma,
            dma,
            dma,
            dma((chunks,)),
            dma,
            dma,
            dma,
            dma,
        ],
        compiler_params=pltpu.CompilerParams(
            collective_id=0, has_side_effects=True, vmem_limit_bytes=48 * 1024 * 1024
        ),
    )(
        cache_table,
        cold_table,
        hit_ids,
        miss_owner.reshape(misses // 128, 128),
        miss_row.reshape(misses // 128, 128),
        history_ids,
        candidate_ids,
        history_len,
        w_kv,
        w_cand,
        w_out,
        w_score.reshape(1, width),
    )


def solution(mesh):
    rows = P(("hst", "dev"), None)
    placed = (
        P("dev", None),
        rows,
        rows,
        rows,
        P(("hst", "dev")),
        rows,
        rows,
        P(("hst", "dev")),
        P(),
        P(),
        P(),
        P(),
    )
    return jax.shard_map(
        functools.partial(per_device, mesh.shape["hst"], mesh.shape["dev"]),
        mesh=mesh,
        in_specs=placed,
        out_specs=rows,
        check_vma=False,
    )
```

time: 202 us -> 102 us (0.50)
  Pallas kernels: 0 us -> 90.7 us
  waiting for transfers between devices: 71.6 us -> 0 us
  blocking collectives: 52.6 us -> 0 us
  local copies, waits for them, and re-layouts: 39.1 us -> 11 us
  starting transfers between devices: 17.6 us -> 0 us
  other arithmetic: 11.7 us -> 0 us
  matrix products: 8.07 us -> 0 us
    pallas_call x0 -> x1, Pallas kernels: none -> 90.7 us  [per_device(): pl.pallas_call(functools.partial(kernel, n_hst, n_dev), out_shape=jax.Sha...]
    all_to_all x3 -> x0, waiting for transfers between devices: 71.6 us -> none  [the longest x1 61.2 us: per_device(): lax.all_to_all(jnp.take(cold_table, lax.all_to_all(request, 'hst', split_...]
    all_to_all x1 -> x0, blocking collectives: 52.6 us -> none  [per_device(): lax.all_to_all(request, 'hst', split_axis=0, concat_axis=0, tiled=True)]
    scatter x1 -> x0, local copies, waits for them, and re-layouts: 21.2 us -> none  [per_device(): jnp.zeros((n_hst, MISS_CAP), jnp.int32).at[owners, slot].set(miss_row)]
    all_to_all x3 -> x0, starting transfers between devices: 17.6 us -> none  [the longest x1 7.09 us: per_device(): lax.all_to_all(jnp.take(cold_table, lax.all_to_all(request, 'hst', split_...]
    gather x5 -> x0, local copies, waits for them, and re-layouts: 12.9 us -> none  [the longest x1 5.07 us: per_device(): history_x = jnp.take(collected, history_ids, axis=0)]
    unnamed x22 -> x25, local copies, waits for them, and re-layouts: 1.49 us -> 11 us
    dot_general x4 -> x0, matrix products: 8.07 us -> none  [the longest x1 2.87 us: block_terms(): jnp.einsum('uhcl,ulhd->uchd', weight, values, preferred_element_type=jnp....]
  transfers between devices with their start and end apart: 3 -> 0, of which waited for: 3 -> 0; matrix products, arithmetic and copies ran while one was open for 4% -> 0% of each run, Pallas kernels for 0% -> 0%
where the time goes in v1:
time: 102 us
  Pallas kernels  90.7 us (89%)
  local copies, waits for them, and re-layouts  11 us (11%)
    pallas_call x1, Pallas kernels, per_device(): pl.pallas_call(functools.partial(kernel, n_hst, n_dev), out_shape=jax.Sha...  90.7 us
    unnamed x25, local copies, waits for them, and re-layouts  11 us

profile of v1, /device:TPU:1, one launch (start us, length us, event | category | flops | bytes accessed | tf_op | source)
XLA Modules:
  0.0 101.7 jit_solution(9207870992616659024)
XLA Ops:
  0.0 0.0 copy-start
  0.0 1.6 %copy-done = bf16[512,2048]{1,0:T(8,128)(2,1)S(1)} copy-done((bf16[512,2048]{1,0:T(8,128)(2,1)S(1)}, bf16[512,2048]{1,0:T(8,128)(2,1)}, u32[]{:S(2)}) %copy-start) | copy-done | bytes 2097176
  1.6 0.0 copy-start.1
  1.6 1.2 %copy-done.1 = bf16[512,1024]{1,0:T(8,128)(2,1)S(1)} copy-done((bf16[512,1024]{1,0:T(8,128)(2,1)S(1)}, bf16[512,1024]{1,0:T(8,128)(2,1)}, u32[]{:S(2)}) %copy-start.1) | copy-done | bytes 1048600
  2.8 0.0 copy-start.2
  2.8 1.0 %copy-done.2 = bf16[512,512]{1,0:T(8,128)(2,1)S(1)} copy-done((bf16[512,512]{1,0:T(8,128)(2,1)S(1)}, bf16[512,512]{1,0:T(8,128)(2,1)}, u32[]{:S(2)}) %copy-start.2) | copy-done | bytes 524312
  3.9 0.0 copy-start.3
  3.9 0.9 copy-done.3
  4.8 0.0 copy-start.4
  4.8 0.8 copy-done.4
  5.7 0.0 copy-start.5
  5.7 0.7 copy-done.5
  6.3 0.0 copy-start.6
  6.3 0.7 copy-done.6
  7.0 0.0 copy-start.7
  7.0 0.7 copy-done.7
  7.7 0.0 copy-start.8
  7.7 0.7 copy-done.8
  8.4 0.0 copy-start.9
  8.4 0.7 copy-done.9
  9.1 0.0 copy-start.10
  9.1 0.7 copy-done.10
  9.8 0.0 copy-start.11
  9.8 0.7 copy-done.11
  10.4 90.7 %shard_map.118 = f32[2,128]{1,0:T(2,128)S(1)} custom-call(bf16[64,512]{1,0:T(8,128)(2,1)S(1)} %copy-done.4, bf16[256,512]{1,0:T(8,128)(2,1)S(1)} %copy-done.3, s32[16,32]{1,0:T(8,128)S(1)} %copy-done.5, s32[2,128]{1,0:T(2,128)S(1)} %bitcast.4, s32[2,128]{1,0:T(2,128)S(1)} %bitcast.5, s32[2,512]{1,0:T(2,128)S(1)} %copy-done.6, s32[2,128]{1,0:T(2,128)S(1)} %copy-done.10, ...), custom_call_target="tpu_custom_call" | custom-call | tf_op jit(solution)/shard_map/pallas_call | solution.py:340
  101.1 0.6 copy.14
Async XLA Ops:
  0.0 1.6 %copy-start = (bf16[512,2048]{1,0:T(8,128)(2,1)S(1)}, bf16[512,2048]{1,0:T(8,128)(2,1)}, u32[]{:S(2)}) copy-start(bf16[512,2048]{1,0:T(8,128)(2,1)} %w_cand_hbm.1) | copy-start | bytes 6291460
  1.6 1.2 %copy-start.1 = (bf16[512,1024]{1,0:T(8,128)(2,1)S(1)}, bf16[512,1024]{1,0:T(8,128)(2,1)}, u32[]{:S(2)}) copy-start(bf16[512,1024]{1,0:T(8,128)(2,1)} %w_kv_hbm.1) | copy-start | bytes 3145732
  2.8 1.0 %copy-start.2 = (bf16[512,512]{1,0:T(8,128)(2,1)S(1)}, bf16[512,512]{1,0:T(8,128)(2,1)}, u32[]{:S(2)}) copy-start(bf16[512,512]{1,0:T(8,128)(2,1)} %w_out_hbm.1) | copy-start | bytes 1572868
  3.9 0.9 copy-start.3
  4.8 0.8 copy-start.4
  5.7 0.7 copy-start.5
  6.3 0.7 copy-start.6
  7.0 0.7 copy-start.7
  7.7 0.7 copy-start.8
  8.4 0.7 copy-start.9
  9.1 0.7 copy-start.10
  9.8 0.7 copy-start.11

commit v2 on v1

v2 whole, which is shorter than its diff:
```python
import functools
import math

import jax
import jax.numpy as jnp
from jax import lax
from jax.experimental import pallas as pl
from jax.experimental.pallas import tpu as pltpu
from jax.sharding import PartitionSpec as P

F32 = jnp.float32
BF16 = jnp.bfloat16
HEADS = 4
DH = 128
CAP = 8
EPS = 1e-05
STARTS = (3, 7, 11, 14)


def iota(shape, dim):
    return lax.broadcasted_iota(jnp.int32, shape, dim)


def normalize(x):
    centered = x - jnp.mean(x, axis=-1, keepdims=True)
    var = jnp.mean(centered * centered, axis=-1, keepdims=True)
    return centered * lax.rsqrt(var + EPS)


def silu_of_double(y):
    return y + y * jnp.tanh(y)


def dot(a, b):
    return jnp.dot(a, b, preferred_element_type=F32)


def dot_nt(a, b):
    return lax.dot_general(a, b, (((1,), (1,)), ((), ())), preferred_element_type=F32)


def columns(rows):
    r, n = rows.shape
    eye = iota((n, n), 0) == iota((n, n), 1)
    spread = jnp.where(eye[None], jnp.broadcast_to(rows[:, None, :], (r, n, n)), 0.0)
    return jnp.sum(spread, axis=-1, keepdims=True).reshape(r * n, 1)


def onehot(column, width):
    lanes = iota((column.shape[0], width), 1).astype(F32)
    return jnp.where(column == lanes, 1.0, 0.0).astype(BF16)


def kernel(
    n_hst,
    n_dev,
    *refs,
):
    inputs, out, held, scratch = refs[:12], refs[12], refs[13:25], refs[25:]
    (cache, cold, hit_ids, owner, miss_row, history_ids, candidate_ids, history_len) = held[:8]
    w_kv, w_cand, w_out, w_score = held[8:]
    (
        asked,
        request,
        reply,
        arrived,
        cached,
        kv,
        load_sem,
        ask_send,
        ask_recv,
        row_send,
        row_recv,
        ag_send,
        ag_recv,
        swap_send,
        swap_recv,
    ) = scratch
    me = lax.axis_index("hst")
    dev = lax.axis_index("dev")
    z, core = me // 2, lax.rem(me, 2)
    nz = n_hst // 2
    far = nz // 2
    hits = hit_ids.shape[0] * hit_ids.shape[1]
    misses = owner.shape[0] * owner.shape[1]
    width = cache.shape[1]
    half_w = width // 2
    users = history_len.shape[0]
    half = cache.shape[0] // 2
    seats = lambda top: 2 + 4 * (far - top - 1) if top < far else 0
    tops = [far] + [max(1, far - n) for n in STARTS]
    chunks = []
    for high, low in zip(tops, tops[1:] + [0]):
        chunks.append((high, low, seats(high), seats(low) if low else n_hst))

    def each_group(high, low, act):
        if high == far:
            chip = lax.rem(z + far, nz)
            act(0, chip, chip, 1 - core)
            act(1, chip, chip, core)
            high = far - 1

        def step(i, carry):
            d = high - i
            up, down = lax.rem(z + d, nz), lax.rem(z + nz - d, nz)
            seat = 2 + 4 * (far - 1 - d)
            act(seat, up, down, 1 - core)
            act(seat + 1, up, down, core)
            act(seat + 2, down, up, 1 - core)
            act(seat + 3, down, up, core)
            return carry

        lax.fori_loop(0, high - max(low, 0), step, 0)
        if low == 0:
            act(n_hst - 2, z, z, 1 - core)

    loads = [
        pltpu.make_async_copy(source, target, load_sem.at[i])
        for i, (source, target) in enumerate(zip(inputs, held))
    ]
    loads[3].start()
    loads[4].start()
    barrier = pltpu.get_barrier_semaphore()

    def greet(seat, chip, back, side):
        pl.semaphore_signal(barrier, inc=1, device_id={"hst": chip * 2 + side, "dev": dev})

    each_group(far, 0, greet)

    def greet_dev(k, carry):
        pl.semaphore_signal(barrier, inc=1, device_id={"hst": me, "dev": lax.rem(dev + k, n_dev)})
        return carry

    lax.fori_loop(1, n_dev, greet_dev, 0)
    for i in (1, 0, 2, 5, 6, 7, 11, 8, 9, 10):
        loads[i].start()

    loads[3].wait()
    loads[4].wait()
    owners = owner[...].astype(F32)
    owner_col = columns(owners)
    row_col = columns(miss_row[...].astype(F32))
    by_miss = onehot(owner_col, 128)
    earlier = jnp.where(iota((misses, misses), 1) < iota((misses, misses), 0), 1.0, 0.0).astype(BF16)
    before = dot(earlier, by_miss)
    slot_col = jnp.sum(before * by_miss.astype(F32), axis=-1, keepdims=True)
    lanes = iota((misses, 128), 1).astype(F32)
    rows_at_slot = jnp.where(slot_col == lanes, row_col, 0.0).astype(BF16)
    wanted = jnp.zeros((n_hst, 128), F32)
    groups = iota((n_hst, 128), 0).astype(F32)
    for i in range(misses // 128):
        by_group = jnp.where(owners[i : i + 1] == groups, 1.0, 0.0).astype(BF16)
        wanted = wanted + dot(by_group, rows_at_slot[i * 128 : (i + 1) * 128])
    asked[...] = wanted.reshape(n_hst, 1, 128)
    request[n_hst - 1] = asked[me]

    pl.semaphore_wait(barrier, n_hst - 1 + n_dev - 1)

    for j, (high, low, _, _) in enumerate(chunks):

        def ask(seat, chip, back, side):
            pltpu.make_async_remote_copy(
                src_ref=asked.at[chip * 2 + side],
                dst_ref=request.at[seat],
                send_sem=ask_send,
                recv_sem=ask_recv.at[j],
                device_id={"hst": chip * 2 + side, "dev": dev},
            ).start()

        each_group(high, low, ask)
    loads[0].wait()

    def share(k, carry):
        pltpu.make_async_remote_copy(
            src_ref=cache.at[pl.ds(pl.multiple_of(core * half, half), half)],
            dst_ref=cached.at[core, k],
            send_sem=ag_send,
            recv_sem=ag_recv,
            device_id={"hst": me, "dev": lax.rem(dev + k, n_dev)},
        ).start()
        return carry

    lax.fori_loop(1, n_dev, share, 0)

    all_but_self = pl.ds(0, n_hst - 1)
    own_group = {"hst": me, "dev": dev}

    def whole(ref, sem_send, sem_recv):
        return pltpu.make_async_remote_copy(
            src_ref=ref, dst_ref=ref, send_sem=sem_send, recv_sem=sem_recv, device_id=own_group
        )

    others = pl.ds(1, n_dev - 1)
    peers, slots = hit_ids.shape

    def count_rows():
        for i in (2, 5, 6, 7):
            loads[i].wait()
        collected = hits + misses
        hist = history_ids.shape[1]
        counts = []
        for u in range(users):
            ids = history_ids[u : u + 1, :].astype(F32)
            ids = jnp.where(iota((1, hist), 1) < history_len[u], ids, -1.0)
            col = jnp.concatenate([columns(ids[:, i * 128 : (i + 1) * 128]) for i in range(hist // 128)], axis=0)
            same = col == iota((hist, collected), 1).astype(F32)
            counts.append(jnp.sum(jnp.where(same, 1.0, 0.0), axis=0, keepdims=True))
        cand_col = columns(candidate_ids[...].astype(F32))
        of_hits = onehot(cand_col, hits)
        of_misses = onehot(cand_col - float(hits), misses)
        return counts, of_hits, of_misses

    def pass_cache():
        whole(cached.at[core, others], ag_send, ag_recv).wait_recv()
        swap = pltpu.make_async_remote_copy(
            src_ref=cached.at[core, others],
            dst_ref=cached.at[core, others],
            send_sem=swap_send,
            recv_sem=swap_recv,
            device_id={"hst": z * 2 + 1 - core, "dev": dev},
        )
        swap.start()
        cached[0, 0] = cache[0:half]
        cached[1, 0] = cache[half:]
        return swap

    def place_hits():
        for i in (8, 9, 10, 11):
            loads[i].wait()
        heads_col = jnp.sum(w_out[...].astype(F32) * w_score[...], axis=-1, keepdims=True)
        eye = iota((128, 128), 0) == iota((128, 128), 1)
        head_row = jnp.concatenate(
            [
                jnp.sum(jnp.where(eye, heads_col[i * 128 : (i + 1) * 128], 0.0), axis=0, keepdims=True)
                for i in range(width // 128)
            ],
            axis=1,
        )
        ids = hit_ids[...]
        peer = iota((peers, slots), 0)
        place = (ids // half) * (peers * half) + lax.rem(dev - peer + peers, peers) * half + lax.rem(ids, half)
        spread = jnp.where(
            (iota((slots, slots), 0) == iota((slots, slots), 1))[None],
            jnp.broadcast_to(place.astype(F32)[:, None, :], (peers, slots, slots)),
            0.0,
        )
        place_col = jnp.sum(spread, axis=-1, keepdims=True).reshape(hits, 1)
        return head_row, place_col

    def take_hits(of_hits, place_col):
        whole(cached.at[1 - core, others], swap_send, swap_recv).wait_recv()
        x_hit = dot(onehot(place_col, 2 * peers * half), cached[...].reshape(2 * peers * half, width)).astype(BF16)
        normed = normalize(x_hit.astype(F32)).astype(BF16)
        kv[0:hits] = silu_of_double(0.5 * dot(normed, w_kv[...])).astype(BF16)
        cand_x = dot(of_hits, x_hit)
        return cand_x

    loads[1].wait()
    for j, (high, low, first, end) in enumerate(chunks):
        n = end - first
        whole(request.at[pl.ds(first, min(end, n_hst - 1) - first)], ask_send, ask_recv.at[j]).wait_recv()
        ids = request[first:end]
        pick = iota((n, CAP, 128), 1) == iota((n, CAP, 128), 2)
        spread = jnp.where(pick, jnp.broadcast_to(ids, (n, CAP, 128)), 0.0)
        col = jnp.sum(spread, axis=-1, keepdims=True).reshape(n * CAP, 1)
        rows = dot(onehot(col, cold.shape[0]), cold[...]).astype(BF16).reshape(n, CAP, width)
        reply[first:end, 0:CAP, :] = rows[:, :, :half_w]
        reply[first:end, CAP:, :] = rows[:, :, half_w:]

        def answer(seat, chip, back, side):
            pltpu.make_async_remote_copy(
                src_ref=reply.at[seat],
                dst_ref=arrived.at[seat],
                send_sem=row_send,
                recv_sem=row_recv.at[j],
                device_id={"hst": back * 2 + side, "dev": dev},
            ).start()

        each_group(high, low, answer)
        if j == 0:
            counts, of_hits, of_misses = count_rows()
            swap = pass_cache()
        if j == 1:
            head_row, place_col = place_hits()
        if j == 2:
            cand_x = take_hits(of_hits, place_col)
    arrived[n_hst - 1] = reply[n_hst - 1]

    o = owner_col.astype(jnp.int32)
    chip = lax.rem(o // 2 - z + nz, nz)
    pair = jnp.where(chip >= far, 2 * (chip - far), 2 * (far - chip) - 1)
    order = 2 * pair + 1 - lax.rem(o + core, 2)
    seat_col = (order * CAP).astype(F32) + slot_col
    left = jnp.zeros((misses, half_w), F32)
    right = jnp.zeros((misses, half_w), F32)
    for j, (_, _, first, end) in enumerate(chunks):
        n = end - first
        whole(arrived.at[pl.ds(first, min(end, n_hst - 1) - first)], row_send, row_recv.at[j]).wait_recv()
        pick = onehot(seat_col - float(first * CAP), n * CAP)
        part = arrived[first:end]
        left = left + dot(pick, part[:, 0:CAP, :].reshape(n * CAP, half_w))
        right = right + dot(pick, part[:, CAP:, :].reshape(n * CAP, half_w))
    x_miss32 = jnp.concatenate([left, right], axis=1)
    x_miss = x_miss32.astype(BF16)
    cand_x = cand_x + dot(of_misses, x_miss)
    normed = normalize(x_miss32).astype(BF16)
    kv[hits:] = silu_of_double(0.5 * dot(normed, w_kv[...])).astype(BF16)

    cand_n = normalize(cand_x).astype(BF16)
    proj = silu_of_double(0.5 * dot(cand_n, w_cand[...])).astype(BF16)
    cands = candidate_ids.shape[1]
    scale = 1.0 / math.sqrt(DH)
    attended = []
    for h in range(HEADS):
        cols = slice(h * DH, (h + 1) * DH)
        at = lambda b: proj[:, b * width + h * DH : b * width + (h + 1) * DH]
        query = at(2)
        half_raw = dot_nt(query, kv[:, cols]) * (0.5 * scale)
        act = silu_of_double(half_raw)
        weight = jnp.concatenate(
            [(act[u * cands : (u + 1) * cands] * counts[u]).astype(BF16) for u in range(users)], axis=0
        )
        summed = dot(weight, kv[:, width + h * DH : width + (h + 1) * DH])
        own = jnp.sum(query.astype(F32) * at(3).astype(F32), axis=-1, keepdims=True) * (0.5 * scale)
        mine = silu_of_double(own) * at(1).astype(F32)
        shares = [
            summed[u * cands : (u + 1) * cands] / history_len[u].astype(F32) for u in range(users)
        ]
        attended.append(jnp.concatenate(shares, axis=0) + mine)
    mixed = normalize(jnp.concatenate(attended, axis=1)) * proj[:, :width].astype(F32)
    score = jnp.sum(cand_x * w_score[...] + mixed * head_row, axis=-1, keepdims=True)
    eye = iota((cands, cands), 0) == iota((cands, cands), 1)
    for u in range(users):
        out[u : u + 1, :] = jnp.sum(
            jnp.where(eye, score[u * cands : (u + 1) * cands], 0.0), axis=0, keepdims=True
        )

    whole(asked.at[all_but_self], ask_send, ask_recv.at[0]).wait_send()
    whole(reply.at[all_but_self], row_send, row_recv.at[0]).wait_send()
    whole(cached.at[core, others], ag_send, ag_recv).wait_send()
    swap.wait_send()


def per_device(
    n_hst,
    n_dev,
    cache_table,
    cold_table,
    hit_ids,
    miss_owner,
    miss_row,
    history_ids,
    candidate_ids,
    history_len,
    w_kv,
    w_cand,
    w_out,
    w_score,
):
    width = cache_table.shape[1]
    misses = miss_row.shape[0]
    collected = hit_ids.size + misses
    half = cache_table.shape[0] // 2
    chunks = 1 + len(STARTS)
    operands = (
        cache_table,
        cold_table,
        hit_ids,
        miss_owner.reshape(misses // 128, 128),
        miss_row.reshape(misses // 128, 128),
        history_ids,
        candidate_ids,
        history_len,
        w_kv,
        w_cand,
        w_out,
        w_score.reshape(1, width),
    )
    spaces = [pltpu.VMEM] * 7 + [pltpu.SMEM] + [pltpu.VMEM] * 4
    dma = pltpu.SemaphoreType.DMA
    return pl.pallas_call(
        functools.partial(kernel, n_hst, n_dev),
        out_shape=jax.ShapeDtypeStruct(candidate_ids.shape, F32),
        in_specs=[pl.BlockSpec(memory_space=pltpu.HBM)] * len(operands),
        out_specs=pl.BlockSpec(memory_space=pltpu.VMEM),
        scratch_shapes=[
            *[space(a.shape, a.dtype) for space, a in zip(spaces, operands)],
            pltpu.VMEM((n_hst, 1, 128), F32),
            pltpu.VMEM((n_hst, 1, 128), F32),
            pltpu.VMEM((n_hst, 2 * CAP, width // 2), BF16),
            pltpu.VMEM((n_hst, 2 * CAP, width // 2), BF16),
            pltpu.VMEM((2, n_dev, half, width), BF16),
            pltpu.VMEM((collected, 2 * width), BF16),
            dma((len(operands),)),
            dma,
            dma((chunks,)),
            dma,
            dma((chunks,)),
            dma,
            dma,
            dma,
            dma,
        ],
        compiler_params=pltpu.CompilerParams(
            collective_id=0, has_side_effects=True, vmem_limit_bytes=48 * 1024 * 1024
        ),
    )(*[pltpu.with_memory_space_constraint(a, pltpu.HBM) for a in operands])


def solution(mesh):
    rows = P(("hst", "dev"), None)
    placed = (
        P("dev", None),
        rows,
        rows,
        rows,
        P(("hst", "dev")),
        rows,
        rows,
        P(("hst", "dev")),
        P(),
        P(),
        P(),
        P(),
    )
    return jax.shard_map(
        functools.partial(per_device, mesh.shape["hst"], mesh.shape["dev"]),
        mesh=mesh,
        in_specs=placed,
        out_specs=rows,
        check_vma=False,
    )
```

time: 102 us -> 90.6 us (0.89)
  local copies, waits for them, and re-layouts: 11 us -> 0.56 us
    unnamed x25 -> x1, local copies, waits for them, and re-layouts: 11 us -> 0.56 us
where the time goes in v2:
time: 90.6 us; the launch traced here: 90.4 us
  Pallas kernels  89.9 us (99%)
    pallas_call x1, Pallas kernels, per_device(): pl.pallas_call(functools.partial(kernel, n_hst, n_dev), out_shape=jax.Sha...  89.9 us

profile of v2, /device:TPU:1, one launch (start us, length us, event | category | flops | bytes accessed | tf_op | source)
XLA Modules:
  0.0 90.4 jit_solution(5635093235736044352)
XLA Ops:
  0.0 89.9 %shard_map.118 = f32[2,128]{1,0:T(2,128)S(1)} custom-call(bf16[64,512]{1,0:T(8,128)(2,1)} %refs_0_.1, bf16[256,512]{1,0:T(8,128)(2,1)} %refs_1_.1, s32[16,32]{1,0:T(8,128)} %refs_2_.1, s32[2,128]{1,0:T(2,128)} %bitcast.4, s32[2,128]{1,0:T(2,128)} %bitcast.5, s32[2,512]{1,0:T(2,128)} %refs_5_.1, s32[2,128]{1,0:T(2,128)} %refs_6_.1, s32[2]{0:T(128)} %refs_7_.1, ...), custom_call_target="tpu_custom_call" | custom-call | tf_op jit(solution)/shard_map/pallas_call | solution.py:381
  89.9 0.6 copy.14

commit v3 on v2

--- a/solution.py
+++ b/solution.py
@@ -15,6 +15,7 @@
 CAP = 8
 EPS = 1e-05
 STARTS = (3, 7, 11, 14)
+ORDER = (4, 3, 0, 1, 2)
 
 
 def iota(shape, dim):
@@ -256,7 +257,8 @@
         return cand_x
 
     loads[1].wait()
-    for j, (high, low, first, end) in enumerate(chunks):
+    for turn, j in enumerate(ORDER):
+        high, low, first, end = chunks[j]
         n = end - first
         whole(request.at[pl.ds(first, min(end, n_hst - 1) - first)], ask_send, ask_recv.at[j]).wait_recv()
         ids = request[first:end]
@@ -277,12 +279,12 @@
             ).start()
 
         each_group(high, low, answer)
-        if j == 0:
+        if turn == 2:
             counts, of_hits, of_misses = count_rows()
             swap = pass_cache()
-        if j == 1:
+        if turn == 3:
             head_row, place_col = place_hits()
-        if j == 2:
+        if turn == 4:
             cand_x = take_hits(of_hits, place_col)
     arrived[n_hst - 1] = reply[n_hst - 1]
 
@@ -293,7 +295,8 @@
     seat_col = (order * CAP).astype(F32) + slot_col
     left = jnp.zeros((misses, half_w), F32)
     right = jnp.zeros((misses, half_w), F32)
-    for j, (_, _, first, end) in enumerate(chunks):
+    for j in ORDER:
+        _, _, first, end = chunks[j]
         n = end - first
         whole(arrived.at[pl.ds(first, min(end, n_hst - 1) - first)], row_send, row_recv.at[j]).wait_recv()
         pick = onehot(seat_col - float(first * CAP), n * CAP)

time: 90.6 us -> 87.2 us (0.962)
  Pallas kernels: 89.9 us -> 86.5 us
    pallas_call x1, Pallas kernels: 89.9 us -> 86.5 us  [per_device(): pl.pallas_call(functools.partial(kernel, n_hst, n_dev), out_shape=jax.Sha...]
where the time goes in v3:
time: 87.2 us; the launch traced here: 87.1 us
  Pallas kernels  86.5 us (99%)
    pallas_call x1, Pallas kernels, per_device(): pl.pallas_call(functools.partial(kernel, n_hst, n_dev), out_shape=jax.Sha...  86.5 us

profile of v3, /device:TPU:1, one launch (start us, length us, event | category | flops | bytes accessed | tf_op | source)
XLA Modules:
  0.0 87.1 jit_solution(1511881132254602294)
XLA Ops:
  0.0 86.5 %shard_map.118 = f32[2,128]{1,0:T(2,128)S(1)} custom-call(bf16[64,512]{1,0:T(8,128)(2,1)} %refs_0_.1, bf16[256,512]{1,0:T(8,128)(2,1)} %refs_1_.1, s32[16,32]{1,0:T(8,128)} %refs_2_.1, s32[2,128]{1,0:T(2,128)} %bitcast.4, s32[2,128]{1,0:T(2,128)} %bitcast.5, s32[2,512]{1,0:T(2,128)} %refs_5_.1, s32[2,128]{1,0:T(2,128)} %refs_6_.1, s32[2]{0:T(128)} %refs_7_.1, ...), custom_call_target="tpu_custom_call" | custom-call | tf_op jit(solution)/shard_map/pallas_call | solution.py:384
  86.5 0.6 copy.14
